TPU v7x, 32 devices: a whole 2x2x4 slice. The times are simulated.
32 devices in a mesh: phase: 4 (over y, x), tile: 4 (over z), dp: 2 (over core).
Axes of the slice: x: 2, y: 2, z: 4, core: 2. Of those that a mesh axis runs over, the one named last changes fastest.
Arguments:
- camera_feats: bfloat16 [4, 2, 3, 4, 176, 128], P(None, 'dp', None, 'tile'), may hold values from -6 to 6
- backbone_w: bfloat16 [4, 1152, 128], P('phase'), may hold values from -0.1875 to 0.1875
- depth_w: bfloat16 [128, 118], replicated, may hold values from -1 to 1
- block_tile: int32 [4, 2, 1056, 1], P('phase', 'dp', 'tile'), may hold values from 0 to 3; in each aligned block of 264 rows (0 to 263, 264 to 527, ..., all dimensions but the last counted through in order) at most 264 rows name the same one
- point_slot: int32 [4, 2, 1056, 236], P('phase', 'dp', 'tile'), may hold values from 0 to 15
- block_cells: int32 [4, 2, 1056, 16], P('phase', 'dp', 'tile'), may hold values from 0 to 1024, as said below
- bev_w: bfloat16 [1152, 128], replicated, may hold values from -0.1875 to 0.1875
- cotangent: bfloat16 [4, 2, 16, 256, 128], P('phase', 'dp', 'tile'), may hold values from -6 to 6
Outputs:
- encoded: bfloat16 [4, 2, 16, 256, 128], P('phase', 'dp', 'tile')
- conv_grad: float32 [128, 1152], P('tile')
Inputs may be any that keep to these rules, and one draw needn't show every extreme that they name: `block_tile`: among the 264 blocks of one sample on one index of tile (an aligned run of rows), at most 264 name the same tile. `block_cells`: 1024 marks a slot whose cell lies outside the grid.
All inputs are finite; a program needn't handle non-finite values.
Results may differ from a plain program's by a relative error of at most 0.0085.
Values may be sent and summed in bfloat16 or wider, within the bound.
A program may use at most 64 MiB of HBM per device.

v0:
```python
import jax
import jax.numpy as jnp
from jax import lax
from jax.sharding import PartitionSpec as P

NSEG = 2
BLK = 4
BOUND = 8.0


def extended(cells, sides, width):
    for axis, dim in sides:
        count = lax.axis_size(axis)
        ends = count - 1
        head = lax.slice_in_dim(cells, 0, width, axis=dim)
        tail = lax.slice_in_dim(cells, cells.shape[dim] - width, cells.shape[dim], axis=dim)
        cells = jnp.concatenate(
            [
                lax.ppermute(tail, axis, [(i, (i + 1) % count) for i in range(ends)]),
                cells,
                lax.ppermute(head, axis, [((i + 1) % count, i) for i in range(ends)]),
            ],
            axis=dim,
        )
    return cells


def passed_along(block, axis, distance):
    devices = range(lax.axis_size(axis))
    route = [(i - distance, i) for i in devices if i - distance in devices]
    return lax.ppermute(block, axis, route)


def from_root(block, axis, source):
    block = jnp.where(lax.axis_index(axis) == source, block, jnp.zeros_like(block))
    return lax.psum(block, axis)


def patches_from(padded, row_count, col_count):
    widened = jnp.pad(padded, [(0, 0)] * (padded.ndim - 2) + [(1, 1), (0, 0)])
    shifted = [
        widened[..., row_off : row_off + row_count, col_off : col_off + col_count, :]
        for row_off in range(3)
        for col_off in range(3)
    ]
    stacked = jnp.concatenate(shifted, axis=-1)
    return stacked.reshape(-1, stacked.shape[-1])


def section(images, weight):
    padded = extended(images, (("tile", 2),), 1)
    hidden = jnp.dot(
        patches_from(padded, images.shape[2], images.shape[3]),
        weight,
        preferred_element_type=jnp.float32,
    ).reshape(images.shape)
    return (images.astype(jnp.float32) + jax.nn.silu(hidden)).astype(jnp.bfloat16)


def body(camera_feats, backbone_w, depth_w, block_tile, point_slot, block_cells, bev_w, cotangent):
    phases = lax.axis_size("phase")
    phase_idx = lax.axis_index("phase")
    tile_count = lax.axis_size("tile")
    micro_all = camera_feats.shape[0]
    per_phase = micro_all // phases
    own_weight = backbone_w[0]
    carried = jnp.zeros_like(camera_feats[0])
    collected = jnp.zeros_like(camera_feats)
    steps_total = micro_all + phases - 1
    for step_idx in range(steps_total):
        if step_idx < micro_all:
            entering = jnp.where(phase_idx == 0, camera_feats[step_idx], carried)
        else:
            entering = carried
        leaving = section(entering, own_weight)
        finished = step_idx - (phases - 1)
        if finished >= 0:
            collected = collected.at[finished].set(
                jnp.where(phase_idx == phases - 1, leaving, collected[finished])
            )
        if step_idx + 1 < steps_total:
            carried = passed_along(leaving, "phase", 1)
    everything = from_root(collected, "phase", phases - 1)
    own_feats = lax.dynamic_slice_in_dim(everything, phase_idx * per_phase, per_phase, 0)
    samples_dev = own_feats.shape[0] * own_feats.shape[1]
    channels = own_feats.shape[-1]
    context = own_feats.reshape(samples_dev, -1, channels)
    positions = context.shape[1]
    seg_len = depth_w.shape[1] // NSEG
    slot_total = block_cells.shape[-1]
    pos_groups = positions // BLK
    block_count = pos_groups * NSEG
    logits = jnp.dot(context.reshape(-1, channels), depth_w, preferred_element_type=jnp.float32)
    depth_prob = jax.nn.softmax(BOUND * jnp.tanh(logits / BOUND), axis=-1)
    depth_blocks = (
        depth_prob.reshape(samples_dev, pos_groups, BLK, NSEG, seg_len)
        .transpose(0, 1, 3, 2, 4)
        .reshape(samples_dev, block_count, BLK, seg_len)
    )
    slot_blocks = point_slot.reshape(samples_dev, block_count, BLK, seg_len)
    splat_w = jnp.stack(
        [
            jnp.sum(
                jnp.where(slot_blocks == target, depth_blocks, jnp.zeros_like(depth_blocks)),
                axis=-1,
            )
            for target in range(slot_total)
        ],
        axis=2,
    ).astype(jnp.bfloat16)
    block_ctx = jnp.repeat(context.reshape(samples_dev, pos_groups, BLK, channels), NSEG, axis=1)
    row_count = cotangent.shape[2]
    col_count = cotangent.shape[3]
    cells_tile = row_count * col_count
    capacity = max(2, 4 * block_count // tile_count)
    targets = block_tile.reshape(samples_dev, block_count)
    member = (targets[..., None] == jnp.arange(tile_count, dtype=jnp.int32)).astype(jnp.int32)
    slot_rank = jnp.sum((jnp.cumsum(member, axis=1) - 1) * member, axis=-1)
    slot_flat = targets * capacity + slot_rank
    sample_rows = jnp.broadcast_to(
        jnp.arange(samples_dev, dtype=jnp.int32)[:, None], slot_flat.shape
    )
    send_ctx = (
        jnp.zeros((samples_dev, tile_count * capacity, BLK, channels), jnp.bfloat16)
        .at[sample_rows, slot_flat]
        .set(block_ctx)
    )
    send_weights = (
        jnp.zeros((samples_dev, tile_count * capacity, slot_total, BLK), jnp.bfloat16)
        .at[sample_rows, slot_flat]
        .set(splat_w)
    )
    send_cells = (
        jnp.full((samples_dev, tile_count * capacity, slot_total), cells_tile, jnp.int32)
        .at[sample_rows, slot_flat]
        .set(block_cells.reshape(samples_dev, block_count, slot_total))
    )
    send_ctx = send_ctx.reshape(samples_dev, tile_count, capacity, BLK, channels)
    send_weights = send_weights.reshape(samples_dev, tile_count, capacity, slot_total, BLK)
    send_cells = send_cells.reshape(samples_dev, tile_count, capacity, slot_total)
    got_ctx, got_weights, got_cells = (
        lax.all_to_all(send_ctx, "tile", split_axis=1, concat_axis=1, tiled=True),
        lax.all_to_all(send_weights, "tile", split_axis=1, concat_axis=1, tiled=True),
        lax.all_to_all(send_cells, "tile", split_axis=1, concat_axis=1, tiled=True),
    )
    pooled = jnp.einsum(
        "ankti,ankic->anktc", got_weights, got_ctx, preferred_element_type=jnp.float32
    ).astype(jnp.bfloat16)
    group_size = min(8, tile_count)
    group_count = tile_count // group_size
    group_rows = group_size * capacity * slot_total
    pooled_groups = jnp.moveaxis(
        pooled.reshape(samples_dev, group_count, group_rows, channels), 1, 0
    )
    cell_groups = jnp.moveaxis(got_cells.reshape(samples_dev, group_count, group_rows), 1, 0)
    cell_range = jnp.arange(cells_tile, dtype=jnp.int32).reshape(1, cells_tile, 1)

    def splat_group(grid_sum, pieces):
        part_pooled, part_cells = pieces
        one_hot = (part_cells[:, None, :] == cell_range).astype(jnp.bfloat16)
        grid_sum = grid_sum + jnp.einsum(
            "sxr,src->sxc", one_hot, part_pooled, preferred_element_type=jnp.float32
        )
        return (grid_sum, None)

    totals, _ = lax.scan(
        splat_group,
        jnp.zeros((samples_dev, cells_tile, channels), jnp.float32),
        (pooled_groups, cell_groups),
    )
    bev_grid = totals.astype(jnp.bfloat16).reshape(samples_dev, row_count, col_count, channels)
    padded_grid = extended(bev_grid, (("tile", 1),), 1)
    bev_patches = patches_from(padded_grid, row_count, col_count)
    mixed = jnp.dot(bev_patches, bev_w, preferred_element_type=jnp.float32)
    encoded = (
        (bev_grid.astype(jnp.float32).reshape(-1, channels) + mixed)
        .astype(jnp.bfloat16)
        .reshape(cotangent.shape)
    )
    upstream = cotangent.reshape(-1, channels)
    total_cells = (
        micro_all * cotangent.shape[1] * lax.axis_size("dp") * row_count * tile_count * col_count
    )
    grad_scale = float(total_cells) ** (-0.5)
    grad_share = lax.psum_scatter(
        grad_scale
        * lax.dot_general(
            upstream, bev_patches, (((0,), (0,)), ((), ())), preferred_element_type=jnp.float32
        ),
        "tile",
        scatter_dimension=0,
        tiled=True,
    )
    conv_grad = lax.psum(grad_share, ("phase", "dp"))
    return (encoded, conv_grad)


def solution(mesh):
    return jax.shard_map(
        body,
        mesh=mesh,
        in_specs=(
            P(None, "dp", None, "tile", None, None),
            P("phase", None, None),
            P(),
            P("phase", "dp", "tile", None),
            P("phase", "dp", "tile", None),
            P("phase", "dp", "tile", None),
            P(),
            P("phase", "dp", "tile", None, None),
        ),
        out_specs=(P("phase", "dp", "tile", None, None), P("tile", None)),
        check_vma=False,
    )
```

profile of v0, /device:TPU:0, one launch (start us, length us, event | category | flops | bytes accessed | tf_op | source)
XLA Modules:
  0.0 385.2 jit_solution(11881665665288128379)
XLA Ops:
  8.2 4.9 %collective-permute-start = (bf16[1,3,1,176,128]{4,3,1,2,0:T(8,128)(2,1)S(1)}, bf16[1,3,1,176,128]{4,3,1,2,0:T(8,128)(2,1)S(1)}, u32[]{:S(2)}, u32[]{:S(2)}) collective-permute-start(bf16[1,3,1,176,128]{4,3,1,2,0:T(8,128)(2,1)S(1)} %fusion.83), channel_id=1, source_target_pairs={{0,2},{2,4},{4,6},{1,3},{3,5},{5,7},{8,10},{10,12},{12,14},{9,11},... | collective-permute-start | bytes 405512 | tf_op jit(solution)/shard_map/ppermute | solution.py:19
  33.8 4.4 %collective-permute-done.4 = bf16[1,3,1,176,128]{4,3,1,2,0:T(8,128)(2,1)S(1)} collective-permute-done((bf16[1,3,1,176,128]{4,3,1,2,0:T(8,128)(2,1)S(1)}, bf16[1,3,1,176,128]{4,3,1,2,0:T(8,128)(2,1)S(1)}, u32[]{:S(2)}, u32[]{:S(2)}) %collective-permute-start.4) | collective-permute-done | bytes 135200 | tf_op jit(solution)/shard_map/ppermute | solution.py:21
  39.3 4.4 %collective-permute-start.5 = (bf16[1,3,1,176,128]{4,3,1,2,0:T(8,128)(2,1)S(1)}, bf16[1,3,1,176,128]{4,3,1,2,0:T(8,128)(2,1)S(1)}, u32[]{:S(2)}, u32[]{:S(2)}) collective-permute-start(bf16[1,3,1,176,128]{4,3,1,2,0:T(8,128)(2,1)S(1)} %add_convert_fusion.5), channel_id=1, source_target_pairs={{0,8},{8,16},{16,24},{1,9},{9,17},{17,25},{2,10},{10,18},{18,26},{... | collective-permute-start | bytes 405512 | tf_op jit(solution)/shard_map/ppermute | solution.py:31
  52.3 4.4 %collective-permute-done.7 = bf16[1,3,1,176,128]{4,3,1,2,0:T(8,128)(2,1)S(1)} collective-permute-done((bf16[1,3,1,176,128]{4,3,1,2,0:T(8,128)(2,1)S(1)}, bf16[1,3,1,176,128]{4,3,1,2,0:T(8,128)(2,1)S(1)}, u32[]{:S(2)}, u32[]{:S(2)}) %collective-permute-start.7) | collective-permute-done | bytes 135200 | tf_op jit(solution)/shard_map/ppermute | solution.py:21
  57.8 4.4 %collective-permute-start.8 = (bf16[1,3,1,176,128]{4,3,1,2,0:T(8,128)(2,1)S(1)}, bf16[1,3,1,176,128]{4,3,1,2,0:T(8,128)(2,1)S(1)}, u32[]{:S(2)}, u32[]{:S(2)}) collective-permute-start(bf16[1,3,1,176,128]{4,3,1,2,0:T(8,128)(2,1)S(1)} %add_convert_fusion.4), channel_id=1, source_target_pairs={{0,8},{8,16},{16,24},{1,9},{9,17},{17,25},{2,10},{10,18},{18,26},{... | collective-permute-start | bytes 405512 | tf_op jit(solution)/shard_map/ppermute | solution.py:31
  66.1 4.6 %collective-permute-start.9 = (bf16[1,3,1,176,128]{4,3,1,2,0:T(8,128)(2,1)S(1)}, bf16[1,3,1,176,128]{4,3,1,2,0:T(8,128)(2,1)S(1)}, u32[]{:S(2)}, u32[]{:S(2)}) collective-permute-start(bf16[1,3,1,176,128]{4,3,1,2,0:T(8,128)(2,1)S(1)} %fusion.57), channel_id=1, source_target_pairs={{0,2},{2,4},{4,6},{1,3},{3,5},{5,7},{8,10},{10,12},{12,14},{9,11},... | collective-permute-start | bytes 405512 | tf_op jit(solution)/shard_map/ppermute | solution.py:19
  74.4 5.2 %collective-permute-start.11 = (bf16[1,3,1,176,128]{4,3,1,2,0:T(8,128)(2,1)S(1)}, bf16[1,3,1,176,128]{4,3,1,2,0:T(8,128)(2,1)S(1)}, u32[]{:S(2)}, u32[]{:S(2)}) collective-permute-start(bf16[1,3,1,176,128]{4,3,1,2,0:T(8,128)(2,1)S(1)} %get-tuple-element.92), channel_id=1, source_target_pairs={{0,8},{8,16},{16,24},{1,9},{9,17},{17,25},{2,10},{10,18},{18,26},{... | collective-permute-start | bytes 405512 | tf_op jit(solution)/shard_map/ppermute | solution.py:31
  82.1 4.4 %collective-permute-start.12 = (bf16[1,3,1,176,128]{4,3,1,2,0:T(8,128)(2,1)S(1)}, bf16[1,3,1,176,128]{4,3,1,2,0:T(8,128)(2,1)S(1)}, u32[]{:S(2)}, u32[]{:S(2)}) collective-permute-start(bf16[1,3,1,176,128]{4,3,1,2,0:T(8,128)(2,1)S(1)} %collective-permute-done.11), channel_id=1, source_target_pairs={{0,2},{2,4},{4,6},{1,3},{3,5},{5,7},{8,10},{10,12},{12,14},{9,11},... | collective-permute-start | bytes 405512 | tf_op jit(solution)/shard_map/ppermute | solution.py:19
  89.0 4.4 %collective-permute-done.13 = bf16[1,3,1,176,128]{4,3,1,2,0:T(8,128)(2,1)S(1)} collective-permute-done((bf16[1,3,1,176,128]{4,3,1,2,0:T(8,128)(2,1)S(1)}, bf16[1,3,1,176,128]{4,3,1,2,0:T(8,128)(2,1)S(1)}, u32[]{:S(2)}, u32[]{:S(2)}) %collective-permute-start.13) | collective-permute-done | bytes 135200 | tf_op jit(solution)/shard_map/ppermute | solution.py:21
  94.6 5.3 %collective-permute-start.14 = (bf16[1,3,1,176,128]{4,3,1,2,0:T(8,128)(2,1)S(1)}, bf16[1,3,1,176,128]{4,3,1,2,0:T(8,128)(2,1)S(1)}, u32[]{:S(2)}, u32[]{:S(2)}) collective-permute-start(bf16[1,3,1,176,128]{4,3,1,2,0:T(8,128)(2,1)S(1)} %get-tuple-element.90), channel_id=1, source_target_pairs={{0,8},{8,16},{16,24},{1,9},{9,17},{17,25},{2,10},{10,18},{18,26},{... | collective-permute-start | bytes 405512 | tf_op jit(solution)/shard_map/ppermute | solution.py:31
  107.1 4.1 %collective-permute-done.16 = bf16[1,3,1,176,128]{4,3,1,2,0:T(8,128)(2,1)S(1)} collective-permute-done((bf16[1,3,1,176,128]{4,3,1,2,0:T(8,128)(2,1)S(1)}, bf16[1,3,1,176,128]{4,3,1,2,0:T(8,128)(2,1)S(1)}, u32[]{:S(2)}, u32[]{:S(2)}) %collective-permute-start.16) | collective-permute-done | bytes 135200 | tf_op jit(solution)/shard_map/ppermute | solution.py:21
  112.4 5.3 %collective-permute-start.17 = (bf16[1,3,1,176,128]{4,3,1,2,0:T(8,128)(2,1)S(1)}, bf16[1,3,1,176,128]{4,3,1,2,0:T(8,128)(2,1)S(1)}, u32[]{:S(2)}, u32[]{:S(2)}) collective-permute-start(bf16[1,3,1,176,128]{4,3,1,2,0:T(8,128)(2,1)S(1)} %get-tuple-element.88), channel_id=1, source_target_pairs={{0,8},{8,16},{16,24},{1,9},{9,17},{17,25},{2,10},{10,18},{18,26},{... | collective-permute-start | bytes 405512 | tf_op jit(solution)/shard_map/ppermute | solution.py:31
  124.7 4.4 %collective-permute-done.19 = bf16[1,3,1,176,128]{4,3,1,2,0:T(8,128)(2,1)S(1)} collective-permute-done((bf16[1,3,1,176,128]{4,3,1,2,0:T(8,128)(2,1)S(1)}, bf16[1,3,1,176,128]{4,3,1,2,0:T(8,128)(2,1)S(1)}, u32[]{:S(2)}, u32[]{:S(2)}) %collective-permute-start.19) | collective-permute-done | bytes 135200 | tf_op jit(solution)/shard_map/ppermute | solution.py:21
  141.2 36.8 %all-reduce.14.cloned.1.call-done = bf16[4,1,3,1,176,128]{5,4,2,3,1,0:T(8,128)(2,1)} async-done(((bf16[4,1,3,1,176,128]{5,4,2,3,1,0:T(8,128)(2,1)}), bf16[4,1,3,1,176,128]{5,4,2,3,1,0:T(8,128)(2,1)}) %all-reduce.14.cloned.1.call-update) | async-done | bytes 540688 | tf_op jit(solution)/shard_map/psum | solution.py:36
  180.1 7.7 %fusion.26 = (bf16[132,2,4]{2,1,0:T(2,128)(2,1)S(1)}, bf16[132,2,4]{2,1,0:T(2,128)(2,1)S(1)}, bf16[132,2,4]{2,1,0:T(2,128)(2,1)S(1)}, bf16[132,2,4]{2,1,0:T(2,12...) fusion(pred[1,132,2,4,59]{4,3,2,1,0:T(4,128)(4,1)S(1)} %eq.411,, ...), kind=kLoop, calls=%fused_computation.54 | loop fusion | flops 1976832 | bytes 1279872 | tf_op jit(solution)/shard_map/reduce_sum | solution.py:103
  202.1 8.6 %scatter_fusion = bf16[1056,16,4]{1,2,0:T(4,128)(2,1)S(1)} fusion(bf16[1056,16,4]{1,2,0:T(4,128)(2,1)S(1)} %broadcast.618, s32[264]{0:T(512)S(1)} %fusion.62, bf16[264,16,4]{1,2,0:T(4,128)(2,1)S(1)} %copy.70), kind=kCustom, calls=%fused_computation.1 | custom fusion | bytes 102432 | tf_op jit(solution)/shard_map/scatter | solution.py:131
  212.0 4.6 %all-to-all-start.1 = ((bf16[1,4,264,16,4]{2,3,4,0,1:T(8,128)(2,1)}), bf16[1,4,264,16,4]{2,3,4,0,1:T(8,128)(2,1)S(1)}, u32[]{:S(2)}, u32[]{:S(2)}) async-start(bf16[1,4,264,16,4]{2,3,4,0,1:T(8,128)(2,1)} %copy.71), calls=%async_computation.1 | async-start | bytes 393216 | tf_op jit(solution)/shard_map/all_to_all | solution.py:143
  217.8 26.7 %scatter_fusion.1 = bf16[1056,4,128]{2,1,0:T(4,128)(2,1)} fusion(bf16[1056,4,128]{2,1,0:T(4,128)(2,1)} %broadcast.620, s32[264]{0:T(512)S(1)} %fusion.62, bf16[264,4,128]{2,1,0:T(4,128)(2,1)S(1)} %bitcast.272), kind=kCustom, calls=%fused_computation.2 | custom fusion | bytes 812064 | tf_op jit(solution)/shard_map/scatter | solution.py:126
  244.6 5.1 %all-to-all-start.2 = ((bf16[1,4,264,4,128]{4,3,2,0,1:T(4,128)(2,1)}), bf16[1,4,264,4,128]{4,3,2,0,1:T(4,128)(2,1)S(1)}, u32[]{:S(2)}, u32[]{:S(2)}) async-start(bf16[1,4,264,4,128]{4,3,2,0,1:T(4,128)(2,1)} %bitcast.70), calls=%async_computation.2 | async-start | bytes 2162688 | tf_op jit(solution)/shard_map/all_to_all | solution.py:142
  250.8 24.5 %all-to-all-done.2 = bf16[1,4,264,4,128]{4,3,2,0,1:T(4,128)(2,1)S(1)} async-done(((bf16[1,4,264,4,128]{4,3,2,0,1:T(4,128)(2,1)}), bf16[1,4,264,4,128]{4,3,2,0,1:T(4,128)(2,1)S(1)}, u32[]{:S(2)}, u32[]{:S(2)}) %all-to-all-start.2) | async-done | bytes 1081376 | tf_op jit(solution)/shard_map/all_to_all | solution.py:142
  277.0 10.5 %fusion.4 = bf16[1024,128]{1,0:T(8,128)(2,1)S(1)} fusion(bf16[16896,128]{1,0:T(8,128)(2,1)S(1)} %bitcast.247, s32[16896]{0:T(1024)S(1)} %eq.358), kind=kOutput, calls=%fused_computation.15 | convolution fusion | flops 4446617600 | bytes 4655104 | tf_op jit(solution)/shard_map/while/body/eval_jaxpr/sxr,src->sxc/dot_general | solution.py:161
  290.8 4.3 %collective-permute-done.21 = bf16[1,1,256,128]{3,2,1,0:T(8,128)(2,1)S(1)} collective-permute-done((bf16[1,1,256,128]{3,2,1,0:T(8,128)(2,1)S(1)}, bf16[1,1,256,128]{3,2,1,0:T(8,128)(2,1)S(1)}, u32[]{:S(2)}, u32[]{:S(2)}) %collective-permute-start.21) | collective-permute-done | bytes 65568 | tf_op jit(solution)/shard_map/ppermute | solution.py:21
  298.7 21.6 %reduce-scatter.4.cloned.1.call-done = f32[32,1152]{1,0:T(8,128)} async-done(((f32[128,1152]{1,0:T(8,128)}), f32[32,1152]{1,0:T(8,128)}) %reduce-scatter.4.cloned.1.call-update) | async-done | bytes 147472
  323.7 53.0 %all-reduce.16.cloned.1.call-done = f32[32,1152]{0,1:T(8,128)} async-done(((f32[32,1152]{0,1:T(8,128)}), f32[32,1152]{0,1:T(8,128)}) %all-reduce.16.cloned.1.call-update) | async-done | bytes 147472 | tf_op jit(solution)/shard_map/psum | solution.py:194
  (232 shorter events, 106.9 us)
Async XLA Ops:
  7.2 170.8 %all-reduce.14.cloned.1.call-start = ((), (), s32[]{:S(2)}) async-start(), calls=%async_computation.4 | async-start | bytes 1081344 | tf_op jit(solution)/shard_map/psum | solution.py:36
  8.2 7.8 %collective-permute-start = (bf16[1,3,1,176,128]{4,3,1,2,0:T(8,128)(2,1)S(1)}, bf16[1,3,1,176,128]{4,3,1,2,0:T(8,128)(2,1)S(1)}, u32[]{:S(2)}, u32[]{:S(2)}) collective-permute-start(bf16[1,3,1,176,128]{4,3,1,2,0:T(8,128)(2,1)S(1)} %fusion.83), channel_id=1, source_target_pairs={{0,2},{2,4},{4,6},{1,3},{3,5},{5,7},{8,10},{10,12},{12,14},{9,11},... | collective-permute-start | bytes 405512 | tf_op jit(solution)/shard_map/ppermute | solution.py:19
  13.1 6.9 %collective-permute-start.1 = (bf16[1,3,1,176,128]{4,3,1,2,0:T(8,128)(2,1)S(1)}, bf16[1,3,1,176,128]{4,3,1,2,0:T(8,128)(2,1)S(1)}, u32[]{:S(2)}, u32[]{:S(2)}) collective-permute-start(bf16[1,3,1,176,128]{4,3,1,2,0:T(8,128)(2,1)S(1)} %fusion.83), channel_id=1, source_target_pairs={{2,0},{4,2},{6,4},{3,1},{5,3},{7,5},{10,8},{12,10},{14,12},{11,9},... | collective-permute-start | bytes 405512 | tf_op jit(solution)/shard_map/ppermute | solution.py:21
  27.8 6.0 %collective-permute-start.3 = (bf16[1,3,1,176,128]{4,3,1,2,0:T(8,128)(2,1)S(1)}, bf16[1,3,1,176,128]{4,3,1,2,0:T(8,128)(2,1)S(1)}, u32[]{:S(2)}, u32[]{:S(2)}) collective-permute-start(bf16[1,3,1,176,128]{4,3,1,2,0:T(8,128)(2,1)S(1)} %fusion.56), channel_id=1, source_target_pairs={{0,2},{2,4},{4,6},{1,3},{3,5},{5,7},{8,10},{10,12},{12,14},{9,11},... | collective-permute-start | bytes 405512 | tf_op jit(solution)/shard_map/ppermute | solution.py:19
  31.3 6.9 %collective-permute-start.4 = (bf16[1,3,1,176,128]{4,3,1,2,0:T(8,128)(2,1)S(1)}, bf16[1,3,1,176,128]{4,3,1,2,0:T(8,128)(2,1)S(1)}, u32[]{:S(2)}, u32[]{:S(2)}) collective-permute-start(bf16[1,3,1,176,128]{4,3,1,2,0:T(8,128)(2,1)S(1)} %fusion.56), channel_id=1, source_target_pairs={{2,0},{4,2},{6,4},{3,1},{5,3},{7,5},{10,8},{12,10},{14,12},{11,9},... | collective-permute-start | bytes 405512 | tf_op jit(solution)/shard_map/ppermute | solution.py:21
  39.3 6.9 %collective-permute-start.5 = (bf16[1,3,1,176,128]{4,3,1,2,0:T(8,128)(2,1)S(1)}, bf16[1,3,1,176,128]{4,3,1,2,0:T(8,128)(2,1)S(1)}, u32[]{:S(2)}, u32[]{:S(2)}) collective-permute-start(bf16[1,3,1,176,128]{4,3,1,2,0:T(8,128)(2,1)S(1)} %add_convert_fusion.5), channel_id=1, source_target_pairs={{0,8},{8,16},{16,24},{1,9},{9,17},{17,25},{2,10},{10,18},{18,26},{... | collective-permute-start | bytes 405512 | tf_op jit(solution)/shard_map/ppermute | solution.py:31
  46.3 6.0 %collective-permute-start.6 = (bf16[1,3,1,176,128]{4,3,1,2,0:T(8,128)(2,1)S(1)}, bf16[1,3,1,176,128]{4,3,1,2,0:T(8,128)(2,1)S(1)}, u32[]{:S(2)}, u32[]{:S(2)}) collective-permute-start(bf16[1,3,1,176,128]{4,3,1,2,0:T(8,128)(2,1)S(1)} %bitcast_select_fusion.16), channel_id=1, source_target_pairs={{0,2},{2,4},{4,6},{1,3},{3,5},{5,7},{8,10},{10,12},{12,14},{9,11},... | collective-permute-start | bytes 405512 | tf_op jit(solution)/shard_map/ppermute | solution.py:19
  49.8 6.9 %collective-permute-start.7 = (bf16[1,3,1,176,128]{4,3,1,2,0:T(8,128)(2,1)S(1)}, bf16[1,3,1,176,128]{4,3,1,2,0:T(8,128)(2,1)S(1)}, u32[]{:S(2)}, u32[]{:S(2)}) collective-permute-start(bf16[1,3,1,176,128]{4,3,1,2,0:T(8,128)(2,1)S(1)} %bitcast_select_fusion.16), channel_id=1, source_target_pairs={{2,0},{4,2},{6,4},{3,1},{5,3},{7,5},{10,8},{12,10},{14,12},{11,9},... | collective-permute-start | bytes 405512 | tf_op jit(solution)/shard_map/ppermute | solution.py:21
  57.8 6.9 %collective-permute-start.8 = (bf16[1,3,1,176,128]{4,3,1,2,0:T(8,128)(2,1)S(1)}, bf16[1,3,1,176,128]{4,3,1,2,0:T(8,128)(2,1)S(1)}, u32[]{:S(2)}, u32[]{:S(2)}) collective-permute-start(bf16[1,3,1,176,128]{4,3,1,2,0:T(8,128)(2,1)S(1)} %add_convert_fusion.4), channel_id=1, source_target_pairs={{0,8},{8,16},{16,24},{1,9},{9,17},{17,25},{2,10},{10,18},{18,26},{... | collective-permute-start | bytes 405512 | tf_op jit(solution)/shard_map/ppermute | solution.py:31
  64.8 6.9 %collective-permute-start.10 = (bf16[1,3,1,176,128]{4,3,1,2,0:T(8,128)(2,1)S(1)}, bf16[1,3,1,176,128]{4,3,1,2,0:T(8,128)(2,1)S(1)}, u32[]{:S(2)}, u32[]{:S(2)}) collective-permute-start(bf16[1,3,1,176,128]{4,3,1,2,0:T(8,128)(2,1)S(1)} %fusion.57), channel_id=1, source_target_pairs={{2,0},{4,2},{6,4},{3,1},{5,3},{7,5},{10,8},{12,10},{14,12},{11,9},... | collective-permute-start | bytes 405512 | tf_op jit(solution)/shard_map/ppermute | solution.py:21
  66.1 7.1 %collective-permute-start.9 = (bf16[1,3,1,176,128]{4,3,1,2,0:T(8,128)(2,1)S(1)}, bf16[1,3,1,176,128]{4,3,1,2,0:T(8,128)(2,1)S(1)}, u32[]{:S(2)}, u32[]{:S(2)}) collective-permute-start(bf16[1,3,1,176,128]{4,3,1,2,0:T(8,128)(2,1)S(1)} %fusion.57), channel_id=1, source_target_pairs={{0,2},{2,4},{4,6},{1,3},{3,5},{5,7},{8,10},{10,12},{12,14},{9,11},... | collective-permute-start | bytes 405512 | tf_op jit(solution)/shard_map/ppermute | solution.py:19
  74.4 7.7 %collective-permute-start.11 = (bf16[1,3,1,176,128]{4,3,1,2,0:T(8,128)(2,1)S(1)}, bf16[1,3,1,176,128]{4,3,1,2,0:T(8,128)(2,1)S(1)}, u32[]{:S(2)}, u32[]{:S(2)}) collective-permute-start(bf16[1,3,1,176,128]{4,3,1,2,0:T(8,128)(2,1)S(1)} %get-tuple-element.92), channel_id=1, source_target_pairs={{0,8},{8,16},{16,24},{1,9},{9,17},{17,25},{2,10},{10,18},{18,26},{... | collective-permute-start | bytes 405512 | tf_op jit(solution)/shard_map/ppermute | solution.py:31
  82.1 6.9 %collective-permute-start.12 = (bf16[1,3,1,176,128]{4,3,1,2,0:T(8,128)(2,1)S(1)}, bf16[1,3,1,176,128]{4,3,1,2,0:T(8,128)(2,1)S(1)}, u32[]{:S(2)}, u32[]{:S(2)}) collective-permute-start(bf16[1,3,1,176,128]{4,3,1,2,0:T(8,128)(2,1)S(1)} %collective-permute-done.11), channel_id=1, source_target_pairs={{0,2},{2,4},{4,6},{1,3},{3,5},{5,7},{8,10},{10,12},{12,14},{9,11},... | collective-permute-start | bytes 405512 | tf_op jit(solution)/shard_map/ppermute | solution.py:19
  86.5 6.9 %collective-permute-start.13 = (bf16[1,3,1,176,128]{4,3,1,2,0:T(8,128)(2,1)S(1)}, bf16[1,3,1,176,128]{4,3,1,2,0:T(8,128)(2,1)S(1)}, u32[]{:S(2)}, u32[]{:S(2)}) collective-permute-start(bf16[1,3,1,176,128]{4,3,1,2,0:T(8,128)(2,1)S(1)} %collective-permute-done.11), channel_id=1, source_target_pairs={{2,0},{4,2},{6,4},{3,1},{5,3},{7,5},{10,8},{12,10},{14,12},{11,9},... | collective-permute-start | bytes 405512 | tf_op jit(solution)/shard_map/ppermute | solution.py:21
  94.6 7.8 %collective-permute-start.14 = (bf16[1,3,1,176,128]{4,3,1,2,0:T(8,128)(2,1)S(1)}, bf16[1,3,1,176,128]{4,3,1,2,0:T(8,128)(2,1)S(1)}, u32[]{:S(2)}, u32[]{:S(2)}) collective-permute-start(bf16[1,3,1,176,128]{4,3,1,2,0:T(8,128)(2,1)S(1)} %get-tuple-element.90), channel_id=1, source_target_pairs={{0,8},{8,16},{16,24},{1,9},{9,17},{17,25},{2,10},{10,18},{18,26},{... | collective-permute-start | bytes 405512 | tf_op jit(solution)/shard_map/ppermute | solution.py:31
  104.3 6.9 %collective-permute-start.16 = (bf16[1,3,1,176,128]{4,3,1,2,0:T(8,128)(2,1)S(1)}, bf16[1,3,1,176,128]{4,3,1,2,0:T(8,128)(2,1)S(1)}, u32[]{:S(2)}, u32[]{:S(2)}) collective-permute-start(bf16[1,3,1,176,128]{4,3,1,2,0:T(8,128)(2,1)S(1)} %collective-permute-done.14), channel_id=1, source_target_pairs={{2,0},{4,2},{6,4},{3,1},{5,3},{7,5},{10,8},{12,10},{14,12},{11,9},... | collective-permute-start | bytes 405512 | tf_op jit(solution)/shard_map/ppermute | solution.py:21
  112.4 7.8 %collective-permute-start.17 = (bf16[1,3,1,176,128]{4,3,1,2,0:T(8,128)(2,1)S(1)}, bf16[1,3,1,176,128]{4,3,1,2,0:T(8,128)(2,1)S(1)}, u32[]{:S(2)}, u32[]{:S(2)}) collective-permute-start(bf16[1,3,1,176,128]{4,3,1,2,0:T(8,128)(2,1)S(1)} %get-tuple-element.88), channel_id=1, source_target_pairs={{0,8},{8,16},{16,24},{1,9},{9,17},{17,25},{2,10},{10,18},{18,26},{... | collective-permute-start | bytes 405512 | tf_op jit(solution)/shard_map/ppermute | solution.py:31
  122.2 6.9 %collective-permute-start.19 = (bf16[1,3,1,176,128]{4,3,1,2,0:T(8,128)(2,1)S(1)}, bf16[1,3,1,176,128]{4,3,1,2,0:T(8,128)(2,1)S(1)}, u32[]{:S(2)}, u32[]{:S(2)}) collective-permute-start(bf16[1,3,1,176,128]{4,3,1,2,0:T(8,128)(2,1)S(1)} %collective-permute-done.17), channel_id=1, source_target_pairs={{2,0},{4,2},{6,4},{3,1},{5,3},{7,5},{10,8},{12,10},{14,12},{11,9},... | collective-permute-start | bytes 405512 | tf_op jit(solution)/shard_map/ppermute | solution.py:21
  133.5 78.5 %all-to-all-start = ((s32[1,4,264,16]{2,3,0,1:T(8,128)}), s32[1,4,264,16]{2,3,0,1:T(8,128)S(1)}, u32[]{:S(2)}, u32[]{:S(2)}) async-start(s32[1,4,264,16]{2,3,0,1:T(8,128)} %copy.48), calls=%async_computation | async-start | bytes 196608 | tf_op jit(solution)/shard_map/all_to_all | solution.py:144
  212.0 32.5 %all-to-all-start.1 = ((bf16[1,4,264,16,4]{2,3,4,0,1:T(8,128)(2,1)}), bf16[1,4,264,16,4]{2,3,4,0,1:T(8,128)(2,1)S(1)}, u32[]{:S(2)}, u32[]{:S(2)}) async-start(bf16[1,4,264,16,4]{2,3,4,0,1:T(8,128)(2,1)} %copy.71), calls=%async_computation.1 | async-start | bytes 393216 | tf_op jit(solution)/shard_map/all_to_all | solution.py:143
  244.6 30.7 %all-to-all-start.2 = ((bf16[1,4,264,4,128]{4,3,2,0,1:T(4,128)(2,1)}), bf16[1,4,264,4,128]{4,3,2,0,1:T(4,128)(2,1)S(1)}, u32[]{:S(2)}, u32[]{:S(2)}) async-start(bf16[1,4,264,4,128]{4,3,2,0,1:T(4,128)(2,1)} %bitcast.70), calls=%async_computation.2 | async-start | bytes 2162688 | tf_op jit(solution)/shard_map/all_to_all | solution.py:142
  249.7 70.6 %reduce-scatter.4.cloned.1.call-start = ((), (), s32[]{:S(2)}) async-start(), calls=%async_computation.6 | async-start | bytes 737280
  288.9 6.2 %collective-permute-start.21 = (bf16[1,1,256,128]{3,2,1,0:T(8,128)(2,1)S(1)}, bf16[1,1,256,128]{3,2,1,0:T(8,128)(2,1)S(1)}, u32[]{:S(2)}, u32[]{:S(2)}) collective-permute-start(bf16[1,1,256,128]{3,2,1,0:T(8,128)(2,1)S(1)} %get-tuple-element.124), channel_id=1, source_target_pairs={{2,0},{4,2},{6,4},{3,1},{5,3},{7,5},{10,8},{12,10},{14,12},{11,9},... | collective-permute-start | bytes 196616 | tf_op jit(solution)/shard_map/ppermute | solution.py:21
  298.6 78.1 %all-reduce.16.cloned.1.call-start = ((), (), s32[]{:S(2)}) async-start(), calls=%async_computation.5 | async-start | bytes 1179648 | tf_op jit(solution)/shard_map/psum | solution.py:194
  (12 other events, 110.6 us)
Sparse Core Ops, SparseCore 0:
  131.3 46.6 all-reduce.13
  298.7 21.4 reduce-scatter.3
  323.4 53.2 all-reduce.15
where the time goes:
time: 387 us; the launch traced here: 385 us
  waiting for transfers between devices  190 us (49%)
  starting transfers between devices  77.4 us (20%)
  local copies, waits for them, and re-layouts  69.9 us (18%)
  matrix products  18.6 us (5%)
  between operations  14.9 us (4%)
  other arithmetic  14.7 us (4%)
    psum x1, waiting for transfers between devices, body(): conv_grad = lax.psum(grad_share, ('phase', 'dp'))  53 us
    psum x1, waiting for transfers between devices, from_root(): return lax.psum(block, axis)  36.8 us
    ppermute x8, waiting for transfers between devices, extended(): lax.ppermute(head, axis, [((i + 1) % count, i) for i in range(ends)])  31.1 us
    ppermute x6, starting transfers between devices, passed_along(): return lax.ppermute(block, axis, route)  27.9 us
    scatter x1, local copies, waits for them, and re-layouts, body(): send_ctx = jnp.zeros((samples_dev, tile_count * capacity, BLK, channels),...  26.7 us
    ppermute x8, starting transfers between devices, extended(): lax.ppermute(tail, axis, [(i, (i + 1) % count) for i in range(ends)])  25.9 us
    all_to_all x1, waiting for transfers between devices, body(): lax.all_to_all(send_ctx, 'tile', split_axis=1, concat_axis=1, tiled=True)  24.5 us
    unnamed x4, waiting for transfers between devices  21.6 us
  transfers between devices with their start and end apart: 28, of which 25 were waited for; matrix products, arithmetic and copies ran while one was open for 19% of the time, Pallas kernels for 0%

commit v1 on v0

--- a/solution.py
+++ b/solution.py
@@ -139,7 +139,12 @@
     send_weights = send_weights.reshape(samples_dev, tile_count, capacity, slot_total, BLK)
     send_cells = send_cells.reshape(samples_dev, tile_count, capacity, slot_total)
     got_ctx, got_weights, got_cells = (
-        lax.all_to_all(send_ctx, "tile", split_axis=1, concat_axis=1, tiled=True),
+        jnp.concatenate(
+            lax.all_to_all(
+                jnp.stack(jnp.split(send_ctx, lax.axis_size("tile"), axis=1)), "tile", 0, 0
+            ),
+            axis=1,
+        ),
         lax.all_to_all(send_weights, "tile", split_axis=1, concat_axis=1, tiled=True),
         lax.all_to_all(send_cells, "tile", split_axis=1, concat_axis=1, tiled=True),
     )

time: 387 us -> 373 us (0.964)
  local copies, waits for them, and re-layouts: 69.9 us -> 51.4 us
  waiting for transfers between devices: 190 us -> 194 us
    scatter x1, local copies, waits for them, and re-layouts: 26.7 us -> 8.62 us  [body(): send_ctx = jnp.zeros((samples_dev, tile_count * capacity, BLK, channels),...]
    all_to_all x1, waiting for transfers between devices: 0.01 us -> 4.93 us  [body(): lax.all_to_all(send_weights, 'tile', split_axis=1, concat_axis=1, tiled=T...]
  transfers between devices with their start and end apart: 28 -> 28, of which waited for: 25 -> 26; matrix products, arithmetic and copies ran while one was open for 19% -> 15% of each run, Pallas kernels for 0% -> 0%
where the time goes in v1:
time: 373 us; the launch traced here: 371 us
  waiting for transfers between devices  194 us (52%)
  starting transfers between devices  75.8 us (20%)
  local copies, waits for them, and re-layouts  51.4 us (14%)
  matrix products  18.6 us (5%)
  other arithmetic  16.7 us (4%)
  between operations  15 us (4%)
    psum x1, waiting for transfers between devices, body(): conv_grad = lax.psum(grad_share, ('phase', 'dp'))  53 us
    psum x1, waiting for transfers between devices, from_root(): return lax.psum(block, axis)  36.8 us
    ppermute x8, waiting for transfers between devices, extended(): lax.ppermute(head, axis, [((i + 1) % count, i) for i in range(ends)])  31.1 us
    ppermute x6, starting transfers between devices, passed_along(): return lax.ppermute(block, axis, route)  27.9 us
    ppermute x8, starting transfers between devices, extended(): lax.ppermute(tail, axis, [(i, (i + 1) % count) for i in range(ends)])  25.9 us
    all_to_all x1, waiting for transfers between devices, body(): lax.all_to_all(jnp.stack(jnp.split(send_ctx, lax.axis_size('tile'), axis=...  23.8 us
    unnamed x4, waiting for transfers between devices  21.6 us
    ppermute x6, waiting for transfers between devices, passed_along(): return lax.ppermute(block, axis, route)  15.1 us
  transfers between devices with their start and end apart: 28, of which 26 were waited for; matrix products, arithmetic and copies ran while one was open for 15% of the time, Pallas kernels for 0%

profile of v1, /device:TPU:0, one launch (start us, length us, event | category | flops | bytes accessed | tf_op | source)
XLA Modules:
  0.0 371.3 jit_solution(10078268077607058202)
XLA Ops:
  8.2 4.9 %collective-permute-start = (bf16[1,3,1,176,128]{4,3,1,2,0:T(8,128)(2,1)S(1)}, bf16[1,3,1,176,128]{4,3,1,2,0:T(8,128)(2,1)S(1)}, u32[]{:S(2)}, u32[]{:S(2)}) collective-permute-start(bf16[1,3,1,176,128]{4,3,1,2,0:T(8,128)(2,1)S(1)} %fusion.83), channel_id=1, source_target_pairs={{0,2},{2,4},{4,6},{1,3},{3,5},{5,7},{8,10},{10,12},{12,14},{9,11},... | collective-permute-start | bytes 405512 | tf_op jit(solution)/shard_map/ppermute | solution.py:19
  33.8 4.4 %collective-permute-done.4 = bf16[1,3,1,176,128]{4,3,1,2,0:T(8,128)(2,1)S(1)} collective-permute-done((bf16[1,3,1,176,128]{4,3,1,2,0:T(8,128)(2,1)S(1)}, bf16[1,3,1,176,128]{4,3,1,2,0:T(8,128)(2,1)S(1)}, u32[]{:S(2)}, u32[]{:S(2)}) %collective-permute-start.4) | collective-permute-done | bytes 135200 | tf_op jit(solution)/shard_map/ppermute | solution.py:21
  39.3 4.4 %collective-permute-start.5 = (bf16[1,3,1,176,128]{4,3,1,2,0:T(8,128)(2,1)S(1)}, bf16[1,3,1,176,128]{4,3,1,2,0:T(8,128)(2,1)S(1)}, u32[]{:S(2)}, u32[]{:S(2)}) collective-permute-start(bf16[1,3,1,176,128]{4,3,1,2,0:T(8,128)(2,1)S(1)} %add_convert_fusion.5), channel_id=1, source_target_pairs={{0,8},{8,16},{16,24},{1,9},{9,17},{17,25},{2,10},{10,18},{18,26},{... | collective-permute-start | bytes 405512 | tf_op jit(solution)/shard_map/ppermute | solution.py:31
  52.3 4.4 %collective-permute-done.7 = bf16[1,3,1,176,128]{4,3,1,2,0:T(8,128)(2,1)S(1)} collective-permute-done((bf16[1,3,1,176,128]{4,3,1,2,0:T(8,128)(2,1)S(1)}, bf16[1,3,1,176,128]{4,3,1,2,0:T(8,128)(2,1)S(1)}, u32[]{:S(2)}, u32[]{:S(2)}) %collective-permute-start.7) | collective-permute-done | bytes 135200 | tf_op jit(solution)/shard_map/ppermute | solution.py:21
  57.8 4.4 %collective-permute-start.8 = (bf16[1,3,1,176,128]{4,3,1,2,0:T(8,128)(2,1)S(1)}, bf16[1,3,1,176,128]{4,3,1,2,0:T(8,128)(2,1)S(1)}, u32[]{:S(2)}, u32[]{:S(2)}) collective-permute-start(bf16[1,3,1,176,128]{4,3,1,2,0:T(8,128)(2,1)S(1)} %add_convert_fusion.4), channel_id=1, source_target_pairs={{0,8},{8,16},{16,24},{1,9},{9,17},{17,25},{2,10},{10,18},{18,26},{... | collective-permute-start | bytes 405512 | tf_op jit(solution)/shard_map/ppermute | solution.py:31
  66.1 4.6 %collective-permute-start.9 = (bf16[1,3,1,176,128]{4,3,1,2,0:T(8,128)(2,1)S(1)}, bf16[1,3,1,176,128]{4,3,1,2,0:T(8,128)(2,1)S(1)}, u32[]{:S(2)}, u32[]{:S(2)}) collective-permute-start(bf16[1,3,1,176,128]{4,3,1,2,0:T(8,128)(2,1)S(1)} %fusion.57), channel_id=1, source_target_pairs={{0,2},{2,4},{4,6},{1,3},{3,5},{5,7},{8,10},{10,12},{12,14},{9,11},... | collective-permute-start | bytes 405512 | tf_op jit(solution)/shard_map/ppermute | solution.py:19
  74.4 5.2 %collective-permute-start.11 = (bf16[1,3,1,176,128]{4,3,1,2,0:T(8,128)(2,1)S(1)}, bf16[1,3,1,176,128]{4,3,1,2,0:T(8,128)(2,1)S(1)}, u32[]{:S(2)}, u32[]{:S(2)}) collective-permute-start(bf16[1,3,1,176,128]{4,3,1,2,0:T(8,128)(2,1)S(1)} %get-tuple-element.92), channel_id=1, source_target_pairs={{0,8},{8,16},{16,24},{1,9},{9,17},{17,25},{2,10},{10,18},{18,26},{... | collective-permute-start | bytes 405512 | tf_op jit(solution)/shard_map/ppermute | solution.py:31
  82.1 4.4 %collective-permute-start.12 = (bf16[1,3,1,176,128]{4,3,1,2,0:T(8,128)(2,1)S(1)}, bf16[1,3,1,176,128]{4,3,1,2,0:T(8,128)(2,1)S(1)}, u32[]{:S(2)}, u32[]{:S(2)}) collective-permute-start(bf16[1,3,1,176,128]{4,3,1,2,0:T(8,128)(2,1)S(1)} %collective-permute-done.11), channel_id=1, source_target_pairs={{0,2},{2,4},{4,6},{1,3},{3,5},{5,7},{8,10},{10,12},{12,14},{9,11},... | collective-permute-start | bytes 405512 | tf_op jit(solution)/shard_map/ppermute | solution.py:19
  89.0 4.4 %collective-permute-done.13 = bf16[1,3,1,176,128]{4,3,1,2,0:T(8,128)(2,1)S(1)} collective-permute-done((bf16[1,3,1,176,128]{4,3,1,2,0:T(8,128)(2,1)S(1)}, bf16[1,3,1,176,128]{4,3,1,2,0:T(8,128)(2,1)S(1)}, u32[]{:S(2)}, u32[]{:S(2)}) %collective-permute-start.13) | collective-permute-done | bytes 135200 | tf_op jit(solution)/shard_map/ppermute | solution.py:21
  94.6 5.3 %collective-permute-start.14 = (bf16[1,3,1,176,128]{4,3,1,2,0:T(8,128)(2,1)S(1)}, bf16[1,3,1,176,128]{4,3,1,2,0:T(8,128)(2,1)S(1)}, u32[]{:S(2)}, u32[]{:S(2)}) collective-permute-start(bf16[1,3,1,176,128]{4,3,1,2,0:T(8,128)(2,1)S(1)} %get-tuple-element.90), channel_id=1, source_target_pairs={{0,8},{8,16},{16,24},{1,9},{9,17},{17,25},{2,10},{10,18},{18,26},{... | collective-permute-start | bytes 405512 | tf_op jit(solution)/shard_map/ppermute | solution.py:31
  107.1 4.1 %collective-permute-done.16 = bf16[1,3,1,176,128]{4,3,1,2,0:T(8,128)(2,1)S(1)} collective-permute-done((bf16[1,3,1,176,128]{4,3,1,2,0:T(8,128)(2,1)S(1)}, bf16[1,3,1,176,128]{4,3,1,2,0:T(8,128)(2,1)S(1)}, u32[]{:S(2)}, u32[]{:S(2)}) %collective-permute-start.16) | collective-permute-done | bytes 135200 | tf_op jit(solution)/shard_map/ppermute | solution.py:21
  112.4 5.3 %collective-permute-start.17 = (bf16[1,3,1,176,128]{4,3,1,2,0:T(8,128)(2,1)S(1)}, bf16[1,3,1,176,128]{4,3,1,2,0:T(8,128)(2,1)S(1)}, u32[]{:S(2)}, u32[]{:S(2)}) collective-permute-start(bf16[1,3,1,176,128]{4,3,1,2,0:T(8,128)(2,1)S(1)} %get-tuple-element.88), channel_id=1, source_target_pairs={{0,8},{8,16},{16,24},{1,9},{9,17},{17,25},{2,10},{10,18},{18,26},{... | collective-permute-start | bytes 405512 | tf_op jit(solution)/shard_map/ppermute | solution.py:31
  124.7 4.4 %collective-permute-done.19 = bf16[1,3,1,176,128]{4,3,1,2,0:T(8,128)(2,1)S(1)} collective-permute-done((bf16[1,3,1,176,128]{4,3,1,2,0:T(8,128)(2,1)S(1)}, bf16[1,3,1,176,128]{4,3,1,2,0:T(8,128)(2,1)S(1)}, u32[]{:S(2)}, u32[]{:S(2)}) %collective-permute-start.19) | collective-permute-done | bytes 135200 | tf_op jit(solution)/shard_map/ppermute | solution.py:21
  141.2 36.8 %all-reduce.14.cloned.1.call-done = bf16[4,1,3,1,176,128]{5,4,2,3,1,0:T(8,128)(2,1)} async-done(((bf16[4,1,3,1,176,128]{5,4,2,3,1,0:T(8,128)(2,1)}), bf16[4,1,3,1,176,128]{5,4,2,3,1,0:T(8,128)(2,1)}) %all-reduce.14.cloned.1.call-update) | async-done | bytes 540688 | tf_op jit(solution)/shard_map/psum | solution.py:36
  180.1 7.7 %fusion.26 = (bf16[132,2,4]{2,1,0:T(2,128)(2,1)S(1)}, bf16[132,2,4]{2,1,0:T(2,128)(2,1)S(1)}, bf16[132,2,4]{2,1,0:T(2,128)(2,1)S(1)}, bf16[132,2,4]{2,1,0:T(2,12...) fusion(pred[1,132,2,4,59]{4,3,2,1,0:T(4,128)(4,1)S(1)} %eq.411,, ...), kind=kLoop, calls=%fused_computation.55 | loop fusion | flops 1976832 | bytes 1279872 | tf_op jit(solution)/shard_map/reduce_sum | solution.py:103
  202.1 8.6 %scatter_fusion = bf16[1056,16,4]{1,2,0:T(4,128)(2,1)S(1)} fusion(bf16[1056,16,4]{1,2,0:T(4,128)(2,1)S(1)} %broadcast.618, s32[264]{0:T(512)S(1)} %fusion.62, bf16[264,16,4]{1,2,0:T(4,128)(2,1)S(1)} %copy.76), kind=kCustom, calls=%fused_computation.1 | custom fusion | bytes 102432 | tf_op jit(solution)/shard_map/scatter | solution.py:131
  212.4 8.6 %scatter_fusion.1 = bf16[1056,4,128]{2,1,0:T(4,128)(2,1)S(1)} fusion(bf16[1056,4,128]{2,1,0:T(4,128)(2,1)S(1)} %broadcast.620, s32[264]{0:T(512)S(1)} %fusion.62, bf16[264,4,128]{2,1,0:T(4,128)(2,1)S(1)} %bitcast.281), kind=kCustom, calls=%fused_computation.2 | custom fusion | bytes 812064 | tf_op jit(solution)/shard_map/scatter | solution.py:126
  221.1 4.6 %all-to-all-start.1 = ((bf16[1,4,264,16,4]{2,3,4,0,1:T(8,128)(2,1)}), bf16[1,4,264,16,4]{2,3,4,0,1:T(8,128)(2,1)S(1)}, u32[]{:S(2)}, u32[]{:S(2)}) async-start(bf16[1,4,264,16,4]{2,3,4,0,1:T(8,128)(2,1)} %copy.77), calls=%async_computation.1 | async-start | bytes 393216 | tf_op jit(solution)/shard_map/all_to_all | solution.py:148
  228.0 4.9 %all-to-all-done.1 = bf16[1,4,264,16,4]{2,3,4,0,1:T(8,128)(2,1)S(1)} async-done(((bf16[1,4,264,16,4]{2,3,4,0,1:T(8,128)(2,1)}), bf16[1,4,264,16,4]{2,3,4,0,1:T(8,128)(2,1)S(1)}, u32[]{:S(2)}, u32[]{:S(2)}) %all-to-all-start.1) | async-done | bytes 135200 | tf_op jit(solution)/shard_map/all_to_all | solution.py:148
  237.6 23.8 %all-to-all-done.2 = bf16[4,1,1,264,4,128]{5,4,3,2,1,0:T(4,128)(2,1)S(1)} async-done(((bf16[4,1,1,264,4,128]{5,4,3,2,1,0:T(4,128)(2,1)}), bf16[4,1,1,264,4,128]{5,4,3,2,1,0:T(4,128)(2,1)S(1)}, u32[]{:S(2)}, u32[]{:S(2)}) %all-to-all-start.2) | async-done | bytes 1081376 | tf_op jit(solution)/shard_map/all_to_all | solution.py:143
  263.2 10.5 %fusion.4 = bf16[1024,128]{1,0:T(8,128)(2,1)S(1)} fusion(bf16[16896,128]{1,0:T(8,128)(2,1)S(1)} %bitcast.256, s32[16896]{0:T(1024)S(1)} %eq.358), kind=kOutput, calls=%fused_computation.15 | convolution fusion | flops 4446617600 | bytes 4655104 | tf_op jit(solution)/shard_map/while/body/eval_jaxpr/sxr,src->sxc/dot_general | solution.py:166
  276.9 4.3 %collective-permute-done.21 = bf16[1,1,256,128]{3,2,1,0:T(8,128)(2,1)S(1)} collective-permute-done((bf16[1,1,256,128]{3,2,1,0:T(8,128)(2,1)S(1)}, bf16[1,1,256,128]{3,2,1,0:T(8,128)(2,1)S(1)}, u32[]{:S(2)}, u32[]{:S(2)}) %collective-permute-start.21) | collective-permute-done | bytes 65568 | tf_op jit(solution)/shard_map/ppermute | solution.py:21
  284.8 21.6 %reduce-scatter.4.cloned.1.call-done = f32[32,1152]{1,0:T(8,128)} async-done(((f32[128,1152]{1,0:T(8,128)}), f32[32,1152]{1,0:T(8,128)}) %reduce-scatter.4.cloned.1.call-update) | async-done | bytes 147472
  309.9 53.0 %all-reduce.16.cloned.1.call-done = f32[32,1152]{0,1:T(8,128)} async-done(((f32[32,1152]{0,1:T(8,128)}), f32[32,1152]{0,1:T(8,128)}) %all-reduce.16.cloned.1.call-update) | async-done | bytes 147472 | tf_op jit(solution)/shard_map/psum | solution.py:199
  (234 shorter events, 112.0 us)
Async XLA Ops:
  7.2 170.8 %all-reduce.14.cloned.1.call-start = ((), (), s32[]{:S(2)}) async-start(), calls=%async_computation.4 | async-start | bytes 1081344 | tf_op jit(solution)/shard_map/psum | solution.py:36
  8.2 7.8 %collective-permute-start = (bf16[1,3,1,176,128]{4,3,1,2,0:T(8,128)(2,1)S(1)}, bf16[1,3,1,176,128]{4,3,1,2,0:T(8,128)(2,1)S(1)}, u32[]{:S(2)}, u32[]{:S(2)}) collective-permute-start(bf16[1,3,1,176,128]{4,3,1,2,0:T(8,128)(2,1)S(1)} %fusion.83), channel_id=1, source_target_pairs={{0,2},{2,4},{4,6},{1,3},{3,5},{5,7},{8,10},{10,12},{12,14},{9,11},... | collective-permute-start | bytes 405512 | tf_op jit(solution)/shard_map/ppermute | solution.py:19
  13.1 6.9 %collective-permute-start.1 = (bf16[1,3,1,176,128]{4,3,1,2,0:T(8,128)(2,1)S(1)}, bf16[1,3,1,176,128]{4,3,1,2,0:T(8,128)(2,1)S(1)}, u32[]{:S(2)}, u32[]{:S(2)}) collective-permute-start(bf16[1,3,1,176,128]{4,3,1,2,0:T(8,128)(2,1)S(1)} %fusion.83), channel_id=1, source_target_pairs={{2,0},{4,2},{6,4},{3,1},{5,3},{7,5},{10,8},{12,10},{14,12},{11,9},... | collective-permute-start | bytes 405512 | tf_op jit(solution)/shard_map/ppermute | solution.py:21
  27.8 6.0 %collective-permute-start.3 = (bf16[1,3,1,176,128]{4,3,1,2,0:T(8,128)(2,1)S(1)}, bf16[1,3,1,176,128]{4,3,1,2,0:T(8,128)(2,1)S(1)}, u32[]{:S(2)}, u32[]{:S(2)}) collective-permute-start(bf16[1,3,1,176,128]{4,3,1,2,0:T(8,128)(2,1)S(1)} %fusion.56), channel_id=1, source_target_pairs={{0,2},{2,4},{4,6},{1,3},{3,5},{5,7},{8,10},{10,12},{12,14},{9,11},... | collective-permute-start | bytes 405512 | tf_op jit(solution)/shard_map/ppermute | solution.py:19
  31.3 6.9 %collective-permute-start.4 = (bf16[1,3,1,176,128]{4,3,1,2,0:T(8,128)(2,1)S(1)}, bf16[1,3,1,176,128]{4,3,1,2,0:T(8,128)(2,1)S(1)}, u32[]{:S(2)}, u32[]{:S(2)}) collective-permute-start(bf16[1,3,1,176,128]{4,3,1,2,0:T(8,128)(2,1)S(1)} %fusion.56), channel_id=1, source_target_pairs={{2,0},{4,2},{6,4},{3,1},{5,3},{7,5},{10,8},{12,10},{14,12},{11,9},... | collective-permute-start | bytes 405512 | tf_op jit(solution)/shard_map/ppermute | solution.py:21
  39.3 6.9 %collective-permute-start.5 = (bf16[1,3,1,176,128]{4,3,1,2,0:T(8,128)(2,1)S(1)}, bf16[1,3,1,176,128]{4,3,1,2,0:T(8,128)(2,1)S(1)}, u32[]{:S(2)}, u32[]{:S(2)}) collective-permute-start(bf16[1,3,1,176,128]{4,3,1,2,0:T(8,128)(2,1)S(1)} %add_convert_fusion.5), channel_id=1, source_target_pairs={{0,8},{8,16},{16,24},{1,9},{9,17},{17,25},{2,10},{10,18},{18,26},{... | collective-permute-start | bytes 405512 | tf_op jit(solution)/shard_map/ppermute | solution.py:31
  46.3 6.0 %collective-permute-start.6 = (bf16[1,3,1,176,128]{4,3,1,2,0:T(8,128)(2,1)S(1)}, bf16[1,3,1,176,128]{4,3,1,2,0:T(8,128)(2,1)S(1)}, u32[]{:S(2)}, u32[]{:S(2)}) collective-permute-start(bf16[1,3,1,176,128]{4,3,1,2,0:T(8,128)(2,1)S(1)} %bitcast_select_fusion.16), channel_id=1, source_target_pairs={{0,2},{2,4},{4,6},{1,3},{3,5},{5,7},{8,10},{10,12},{12,14},{9,11},... | collective-permute-start | bytes 405512 | tf_op jit(solution)/shard_map/ppermute | solution.py:19
  49.8 6.9 %collective-permute-start.7 = (bf16[1,3,1,176,128]{4,3,1,2,0:T(8,128)(2,1)S(1)}, bf16[1,3,1,176,128]{4,3,1,2,0:T(8,128)(2,1)S(1)}, u32[]{:S(2)}, u32[]{:S(2)}) collective-permute-start(bf16[1,3,1,176,128]{4,3,1,2,0:T(8,128)(2,1)S(1)} %bitcast_select_fusion.16), channel_id=1, source_target_pairs={{2,0},{4,2},{6,4},{3,1},{5,3},{7,5},{10,8},{12,10},{14,12},{11,9},... | collective-permute-start | bytes 405512 | tf_op jit(solution)/shard_map/ppermute | solution.py:21
  57.8 6.9 %collective-permute-start.8 = (bf16[1,3,1,176,128]{4,3,1,2,0:T(8,128)(2,1)S(1)}, bf16[1,3,1,176,128]{4,3,1,2,0:T(8,128)(2,1)S(1)}, u32[]{:S(2)}, u32[]{:S(2)}) collective-permute-start(bf16[1,3,1,176,128]{4,3,1,2,0:T(8,128)(2,1)S(1)} %add_convert_fusion.4), channel_id=1, source_target_pairs={{0,8},{8,16},{16,24},{1,9},{9,17},{17,25},{2,10},{10,18},{18,26},{... | collective-permute-start | bytes 405512 | tf_op jit(solution)/shard_map/ppermute | solution.py:31
  64.8 6.9 %collective-permute-start.10 = (bf16[1,3,1,176,128]{4,3,1,2,0:T(8,128)(2,1)S(1)}, bf16[1,3,1,176,128]{4,3,1,2,0:T(8,128)(2,1)S(1)}, u32[]{:S(2)}, u32[]{:S(2)}) collective-permute-start(bf16[1,3,1,176,128]{4,3,1,2,0:T(8,128)(2,1)S(1)} %fusion.57), channel_id=1, source_target_pairs={{2,0},{4,2},{6,4},{3,1},{5,3},{7,5},{10,8},{12,10},{14,12},{11,9},... | collective-permute-start | bytes 405512 | tf_op jit(solution)/shard_map/ppermute | solution.py:21
  66.1 7.1 %collective-permute-start.9 = (bf16[1,3,1,176,128]{4,3,1,2,0:T(8,128)(2,1)S(1)}, bf16[1,3,1,176,128]{4,3,1,2,0:T(8,128)(2,1)S(1)}, u32[]{:S(2)}, u32[]{:S(2)}) collective-permute-start(bf16[1,3,1,176,128]{4,3,1,2,0:T(8,128)(2,1)S(1)} %fusion.57), channel_id=1, source_target_pairs={{0,2},{2,4},{4,6},{1,3},{3,5},{5,7},{8,10},{10,12},{12,14},{9,11},... | collective-permute-start | bytes 405512 | tf_op jit(solution)/shard_map/ppermute | solution.py:19
  74.4 7.7 %collective-permute-start.11 = (bf16[1,3,1,176,128]{4,3,1,2,0:T(8,128)(2,1)S(1)}, bf16[1,3,1,176,128]{4,3,1,2,0:T(8,128)(2,1)S(1)}, u32[]{:S(2)}, u32[]{:S(2)}) collective-permute-start(bf16[1,3,1,176,128]{4,3,1,2,0:T(8,128)(2,1)S(1)} %get-tuple-element.92), channel_id=1, source_target_pairs={{0,8},{8,16},{16,24},{1,9},{9,17},{17,25},{2,10},{10,18},{18,26},{... | collective-permute-start | bytes 405512 | tf_op jit(solution)/shard_map/ppermute | solution.py:31
  82.1 6.9 %collective-permute-start.12 = (bf16[1,3,1,176,128]{4,3,1,2,0:T(8,128)(2,1)S(1)}, bf16[1,3,1,176,128]{4,3,1,2,0:T(8,128)(2,1)S(1)}, u32[]{:S(2)}, u32[]{:S(2)}) collective-permute-start(bf16[1,3,1,176,128]{4,3,1,2,0:T(8,128)(2,1)S(1)} %collective-permute-done.11), channel_id=1, source_target_pairs={{0,2},{2,4},{4,6},{1,3},{3,5},{5,7},{8,10},{10,12},{12,14},{9,11},... | collective-permute-start | bytes 405512 | tf_op jit(solution)/shard_map/ppermute | solution.py:19
  86.5 6.9 %collective-permute-start.13 = (bf16[1,3,1,176,128]{4,3,1,2,0:T(8,128)(2,1)S(1)}, bf16[1,3,1,176,128]{4,3,1,2,0:T(8,128)(2,1)S(1)}, u32[]{:S(2)}, u32[]{:S(2)}) collective-permute-start(bf16[1,3,1,176,128]{4,3,1,2,0:T(8,128)(2,1)S(1)} %collective-permute-done.11), channel_id=1, source_target_pairs={{2,0},{4,2},{6,4},{3,1},{5,3},{7,5},{10,8},{12,10},{14,12},{11,9},... | collective-permute-start | bytes 405512 | tf_op jit(solution)/shard_map/ppermute | solution.py:21
  94.6 7.8 %collective-permute-start.14 = (bf16[1,3,1,176,128]{4,3,1,2,0:T(8,128)(2,1)S(1)}, bf16[1,3,1,176,128]{4,3,1,2,0:T(8,128)(2,1)S(1)}, u32[]{:S(2)}, u32[]{:S(2)}) collective-permute-start(bf16[1,3,1,176,128]{4,3,1,2,0:T(8,128)(2,1)S(1)} %get-tuple-element.90), channel_id=1, source_target_pairs={{0,8},{8,16},{16,24},{1,9},{9,17},{17,25},{2,10},{10,18},{18,26},{... | collective-permute-start | bytes 405512 | tf_op jit(solution)/shard_map/ppermute | solution.py:31
  104.3 6.9 %collective-permute-start.16 = (bf16[1,3,1,176,128]{4,3,1,2,0:T(8,128)(2,1)S(1)}, bf16[1,3,1,176,128]{4,3,1,2,0:T(8,128)(2,1)S(1)}, u32[]{:S(2)}, u32[]{:S(2)}) collective-permute-start(bf16[1,3,1,176,128]{4,3,1,2,0:T(8,128)(2,1)S(1)} %collective-permute-done.14), channel_id=1, source_target_pairs={{2,0},{4,2},{6,4},{3,1},{5,3},{7,5},{10,8},{12,10},{14,12},{11,9},... | collective-permute-start | bytes 405512 | tf_op jit(solution)/shard_map/ppermute | solution.py:21
  112.4 7.8 %collective-permute-start.17 = (bf16[1,3,1,176,128]{4,3,1,2,0:T(8,128)(2,1)S(1)}, bf16[1,3,1,176,128]{4,3,1,2,0:T(8,128)(2,1)S(1)}, u32[]{:S(2)}, u32[]{:S(2)}) collective-permute-start(bf16[1,3,1,176,128]{4,3,1,2,0:T(8,128)(2,1)S(1)} %get-tuple-element.88), channel_id=1, source_target_pairs={{0,8},{8,16},{16,24},{1,9},{9,17},{17,25},{2,10},{10,18},{18,26},{... | collective-permute-start | bytes 405512 | tf_op jit(solution)/shard_map/ppermute | solution.py:31
  122.2 6.9 %collective-permute-start.19 = (bf16[1,3,1,176,128]{4,3,1,2,0:T(8,128)(2,1)S(1)}, bf16[1,3,1,176,128]{4,3,1,2,0:T(8,128)(2,1)S(1)}, u32[]{:S(2)}, u32[]{:S(2)}) collective-permute-start(bf16[1,3,1,176,128]{4,3,1,2,0:T(8,128)(2,1)S(1)} %collective-permute-done.17), channel_id=1, source_target_pairs={{2,0},{4,2},{6,4},{3,1},{5,3},{7,5},{10,8},{12,10},{14,12},{11,9},... | collective-permute-start | bytes 405512 | tf_op jit(solution)/shard_map/ppermute | solution.py:21
  133.5 87.5 %all-to-all-start = ((s32[1,4,264,16]{2,3,0,1:T(8,128)}), s32[1,4,264,16]{2,3,0,1:T(8,128)S(1)}, u32[]{:S(2)}, u32[]{:S(2)}) async-start(s32[1,4,264,16]{2,3,0,1:T(8,128)} %copy.54), calls=%async_computation | async-start | bytes 196608 | tf_op jit(solution)/shard_map/all_to_all | solution.py:149
  221.1 11.9 %all-to-all-start.1 = ((bf16[1,4,264,16,4]{2,3,4,0,1:T(8,128)(2,1)}), bf16[1,4,264,16,4]{2,3,4,0,1:T(8,128)(2,1)S(1)}, u32[]{:S(2)}, u32[]{:S(2)}) async-start(bf16[1,4,264,16,4]{2,3,4,0,1:T(8,128)(2,1)} %copy.77), calls=%async_computation.1 | async-start | bytes 393216 | tf_op jit(solution)/shard_map/all_to_all | solution.py:148
  233.0 28.5 %all-to-all-start.2 = ((bf16[4,1,1,264,4,128]{5,4,3,2,1,0:T(4,128)(2,1)}), bf16[4,1,1,264,4,128]{5,4,3,2,1,0:T(4,128)(2,1)S(1)}, u32[]{:S(2)}, u32[]{:S(2)}) async-start(bf16[4,1,1,264,4,128]{5,4,3,2,1,0:T(4,128)(2,1)} %pad_maximum_fusion), calls=%async_computation.2 | async-start | bytes 2162688 | tf_op jit(solution)/shard_map/all_to_all | solution.py:143
  236.5 69.9 %reduce-scatter.4.cloned.1.call-start = ((), (), s32[]{:S(2)}) async-start(), calls=%async_computation.6 | async-start | bytes 737280
  275.0 6.2 %collective-permute-start.21 = (bf16[1,1,256,128]{3,2,1,0:T(8,128)(2,1)S(1)}, bf16[1,1,256,128]{3,2,1,0:T(8,128)(2,1)S(1)}, u32[]{:S(2)}, u32[]{:S(2)}) collective-permute-start(bf16[1,1,256,128]{3,2,1,0:T(8,128)(2,1)S(1)} %get-tuple-element.128), channel_id=1, source_target_pairs={{2,0},{4,2},{6,4},{3,1},{5,3},{7,5},{10,8},{12,10},{14,12},{11,9},... | collective-permute-start | bytes 196616 | tf_op jit(solution)/shard_map/ppermute | solution.py:21
  284.8 78.1 %all-reduce.16.cloned.1.call-start = ((), (), s32[]{:S(2)}) async-start(), calls=%async_computation.5 | async-start | bytes 1179648 | tf_op jit(solution)/shard_map/psum | solution.py:199
  (12 other events, 110.6 us)
Sparse Core Ops, SparseCore 0:
  131.3 46.6 all-reduce.13
  284.9 21.4 reduce-scatter.3
  309.5 53.2 all-reduce.15
